TPU v7x, 256 devices: a whole 4x4x8 slice. The times are simulated.
256 devices in a mesh: seq: 4 (over x), vocab: 64 (over y, z, core).
Axes of the slice: x: 4, y: 4, z: 8, core: 2. Of those that a mesh axis runs over, the one named last changes fastest.
Arguments:
- teacher_hidden: bfloat16 [1024, 8192], P(None, 'seq'), may hold values from -480 to 480
- teacher_head: bfloat16 [8192, 81920], P('seq', 'vocab'), may hold values from -1 to 1
- student_hidden: bfloat16 [1024, 3584], P(None, 'seq'), may hold values from -480 to 480
- student_head: bfloat16 [3584, 81920], P('seq', 'vocab'), may hold values from -1 to 1
- kept: int32 [8, 64], replicated, may hold values from 0 to 639, as said below
Outputs:
- loss_rows: float32 [1024], P('seq')
- hidden_grad: bfloat16 [1024, 3584], P('vocab', 'seq')
- head_grad: bfloat16 [3584, 81920], P('seq', 'vocab')
Inputs may be any that keep to these rules, and one draw needn't show every extreme that they name: `kept`: each row holds 64 distinct block ids in ascending order. In every row at most 4 of them lie within one run of 10 consecutive blocks starting at a multiple of 10, and in every row some such run holds exactly 4.
All inputs are finite; a program needn't handle non-finite values.
Results may differ from a plain program's by a relative error of at most 0.0049.
Values may be sent and summed in bfloat16 or wider, within the bound.
No kernel may reach another device: no remote copies, remote signals or barrier semaphores. Data moves between devices by JAX's collectives and lax.ppermute only.
A program may use at most 128 MiB of HBM per device.

v0:
```python
import jax
import jax.numpy as jnp
from jax import lax
from jax.sharding import Mesh
from jax.sharding import PartitionSpec as P

BLOCK = 128
VOCAB = ("vocab_0", "vocab_1", "vocab_2")


masked_value = -1e30
loss_scale = 2048.0


def in_blocks(array, dim, devices):
    before, after = (array.shape[:dim], array.shape[dim + 1 :])
    return jnp.moveaxis(array.reshape(*before, devices, -1, *after), dim, 0)


def sent_and_summed(array, axis, dim):
    tiles = in_blocks(array, dim, lax.axis_size(axis))
    arrived = lax.all_to_all(tiles, axis, split_axis=0, concat_axis=0, tiled=True)
    return arrived.sum(axis=0)


def sent_to_all(array, axis):
    devices = lax.axis_size(axis)
    return lax.all_to_all(
        jnp.broadcast_to(array[None], (devices, *array.shape)), axis, 0, 0, tiled=True
    )


def all_in_one(array, axis):
    leaves = jax.tree.leaves(array)
    sequence = sorted(range(len(leaves)), key=lambda k: -leaves[k].size)
    width = (1, *leaves[sequence[0]].shape)[-1]
    lines = [
        jnp.pad(leaves[k].reshape(-1), (0, -leaves[k].size % width)).reshape(-1, width)
        for k in sequence
    ]
    both, at, found = (sent_to_all(jnp.concatenate(lines), axis), 0, {})
    for k, line in zip(sequence, lines):
        piece = both[:, at : at + len(line)].reshape(len(both), -1)
        found[k] = piece[:, : leaves[k].size].reshape(-1, *leaves[k].shape)
        at += len(line)
    numbers = iter(range(len(leaves)))
    return jax.tree.map(lambda _: found[next(numbers)], array)


def combined_pairwise(pieces, combine):
    while len(jax.tree.leaves(pieces)[0]) > 1:
        pieces = jax.vmap(combine)(
            *(jax.tree.map(lambda part: part[side::2], pieces) for side in (0, 1))
        )
    return jax.tree.map(lambda part: part[0], pieces)


def joined_all(array, axis, combine):
    pieces = all_in_one(array, axis)
    return combined_pairwise(pieces, combine)


def joined_along(tiles, dim):
    lengths = list(tiles.shape[1:])
    lengths[dim] *= tiles.shape[0]
    return jnp.moveaxis(tiles, 0, dim).reshape(lengths)


def gather_directly(array, axis, dim):
    tiles = sent_to_all(array, axis)
    return joined_along(tiles, dim)


def sum_by_axis(array, axes, dim):
    far, near = axes
    tiles = in_blocks(array, dim, lax.axis_size(far))
    nearer = sent_and_summed(tiles, near, dim + 1)
    arrived = lax.all_to_all(nearer, far, split_axis=0, concat_axis=0, tiled=True)
    return arrived.sum(axis=0)


def combine_stats(former, latter):
    teacher_top = jnp.maximum(former[0], latter[0])
    former_teacher = jnp.exp(former[0] - teacher_top)
    latter_teacher = jnp.exp(latter[0] - teacher_top)
    student_top = jnp.maximum(former[4], latter[4])
    former_student = jnp.exp(former[4] - student_top)
    latter_student = jnp.exp(latter[4] - student_top)
    return (
        teacher_top,
        former[1] * former_teacher + latter[1] * latter_teacher,
        former[2] * former_teacher + latter[2] * latter_teacher,
        former[3] * former_teacher + latter[3] * latter_teacher,
        student_top,
        former[5] * former_student + latter[5] * latter_student,
    )


def body(teacher_hidden, teacher_head, student_hidden, student_head, kept):
    tokens_all = teacher_hidden.shape[0]
    teacher_part = teacher_hidden.shape[1]
    vocab_cols = teacher_head.shape[1]
    blocks_dev = vocab_cols // BLOCK
    group_rows = tokens_all // lax.axis_size("seq")
    local_blocks = group_rows // BLOCK
    all_blocks = tokens_all // BLOCK
    seq_index = lax.axis_index("seq")
    vocab_index = lax.axis_index(VOCAB)
    first_block = vocab_index * blocks_dev
    block_ids = first_block + jnp.arange(blocks_dev, dtype=jnp.int32)
    my_kept = lax.dynamic_slice_in_dim(kept, seq_index * local_blocks, local_blocks, 0)
    keep_blocks = jnp.any(my_kept[:, :, None] == block_ids[None, None, :], axis=1)
    keep_mask = jnp.broadcast_to(
        keep_blocks[:, None, :, None], (local_blocks, BLOCK, blocks_dev, BLOCK)
    ).reshape(group_rows, vocab_cols)
    kept_count = kept.shape[1]
    most_local = min(blocks_dev, max(4, kept_count // lax.axis_size(VOCAB)))
    before = jnp.sum((kept < first_block).astype(jnp.int32), axis=1)
    slot_index = before[:, None] + jnp.arange(most_local, dtype=jnp.int32)[None, :]
    slot_ids = jnp.take_along_axis(kept, jnp.minimum(slot_index, kept_count - 1), axis=1)
    local_ids = slot_ids - first_block
    slot_valid = (slot_index < kept_count) & (local_ids >= 0) & (local_ids < blocks_dev)
    safe_ids = jnp.clip(local_ids, 0, blocks_dev - 1)
    head_blocks = teacher_head.reshape(teacher_part, blocks_dev, BLOCK)
    picked = jnp.take(head_blocks, safe_ids, axis=1)
    hidden_blocks = teacher_hidden.reshape(all_blocks, BLOCK, teacher_part)
    partial_value = jnp.einsum(
        "rtd,drmc->rtmc", hidden_blocks, picked, preferred_element_type=jnp.float32
    )
    compact = sent_and_summed(partial_value, "seq", 0)
    my_valid = lax.dynamic_slice_in_dim(slot_valid, seq_index * local_blocks, local_blocks, 0)
    my_ids = lax.dynamic_slice_in_dim(safe_ids, seq_index * local_blocks, local_blocks, 0)
    placer = (
        (my_ids[:, :, None] == jnp.arange(blocks_dev, dtype=jnp.int32)[None, None, :])
        & my_valid[:, :, None]
    ).astype(jnp.float32)
    teacher_logits = jnp.einsum(
        "rtmc,rmb->rtbc", compact, placer, precision=lax.Precision.HIGHEST
    ).reshape(group_rows, vocab_cols)
    student_logits = lax.psum_scatter(
        jnp.dot(student_hidden, student_head, preferred_element_type=jnp.float32),
        "seq",
        scatter_dimension=0,
        tiled=True,
    )
    local_top = jnp.max(jnp.where(keep_mask, teacher_logits, masked_value), axis=1)
    weights = jnp.where(keep_mask, jnp.exp(teacher_logits - local_top[:, None]), 0.0)
    local_total = jnp.sum(weights, axis=1)
    local_cross = jnp.sum(weights * student_logits, axis=1)
    local_self = jnp.sum(weights * teacher_logits, axis=1)
    student_top = jnp.max(student_logits, axis=1)
    student_local = jnp.sum(jnp.exp(student_logits - student_top[:, None]), axis=1)
    merged = joined_all(
        (local_top, local_total, local_cross, local_self, student_top, student_local),
        VOCAB,
        combine_stats,
    )
    teacher_max, teacher_total, cross_total, self_total, student_max, student_total = merged
    loss_rows = (
        self_total / teacher_total
        - teacher_max
        - jnp.log(teacher_total)
        - (cross_total / teacher_total - student_max - jnp.log(student_total))
    )
    teacher_prob = (
        jnp.where(keep_mask, jnp.exp(teacher_logits - teacher_max[:, None]), 0.0)
        / teacher_total[:, None]
    )
    student_prob = jnp.exp(student_logits - student_max[:, None]) / student_total[:, None]
    grad_logits = (loss_scale * (student_prob - teacher_prob)).astype(jnp.bfloat16)
    grad_piece = gather_directly(grad_logits, "seq", 0)
    head_total = lax.dot_general(
        student_hidden, grad_piece, (((0,), (0,)), ((), ())), preferred_element_type=jnp.float32
    )
    piece_grad = lax.dot_general(
        grad_piece, student_head, (((1,), (1,)), ((), ())), preferred_element_type=jnp.float32
    )
    hidden_total = piece_grad
    head_total, hidden_total = (head_total, hidden_total)
    hidden_grad = sum_by_axis(hidden_total, (("vocab_0", "vocab_1"), "vocab_2"), 0).astype(
        jnp.bfloat16
    )
    return (loss_rows, hidden_grad, head_total.astype(jnp.bfloat16))


def solution(mesh):
    split = Mesh(
        mesh.devices.reshape(mesh.shape["seq"], 4, 8, 2), ("seq", "vocab_0", "vocab_1", "vocab_2")
    )
    in_specs = (P(None, "seq"), P("seq", VOCAB), P(None, "seq"), P("seq", VOCAB), P())
    out_specs = (P("seq"), P(VOCAB, "seq"), P("seq", VOCAB))
    return jax.shard_map(body, mesh=split, in_specs=in_specs, out_specs=out_specs, check_vma=False)
```

profile of v0, /device:TPU:1, one launch (start us, length us, event | category | flops | bytes accessed | tf_op | source)
XLA Modules:
  0.0 264.8 jit_solution(1725014855212451705)
XLA Ops:
  7.2 1.6 copy-done
  8.8 6.8 %fusion.47 = f32[1024,1280]{1,0:T(8,128)} fusion(bf16[1024,896]{1,0:T(8,128)(2,1)} %param.7, bf16[896,1280]{1,0:T(8,128)(2,1)S(1)} %copy-done), kind=kOutput, calls=%fused_computation.119 | convolution fusion | flops 2348810240 | bytes 9371648 | tf_op jit(solution)/shard_map/dot_general | solution.py:141
  15.6 0.7 copy-done.1
  16.5 0.7 gather_fusion.1
  17.4 8.0 %copy.38 = bf16[2048,1280]{0,1:T(8,128)(2,1)} copy(bf16[2048,1280]{1,0:T(8,128)(2,1)} %param.6) | data formatting | bytes 10485760 | tf_op args[1]
  25.3 8.1 %copy.39 = bf16[2048,10,128]{2,0,1:T(8,128)(2,1)} copy(bf16[2048,10,128]{0,2,1:T(8,128)(2,1)} %bitcast.120) | data formatting | bytes 10485760 | tf_op jit(solution)/shard_map/reshape | solution.py:124
  33.6 9.6 %gather_fusion = bf16[32,2048,128]{2,1,0:T(8,128)(2,1)} fusion(bf16[2048,10,128]{2,0,1:T(8,128)(2,1)} %copy.39, s32[1024]{0:T(1024)S(1)} %pad_clamp_fusion), kind=kCustom, calls=%fused_computation | custom fusion | bytes 33554560 | tf_op jit(solution)/shard_map/jit(_take)/gather | solution.py:125
  43.2 21.8 %copy.40 = bf16[8,4,2048,128]{2,3,1,0:T(8,128)(2,1)} copy(bf16[8,4,2048,128]{3,2,1,0:T(8,128)(2,1)} %bitcast.117) | data formatting | bytes 33554432 | tf_op jit(solution)/shard_map/jit(_take)/gather | solution.py:125
  65.1 10.6 %fusion = f32[8,4,128,128]{3,2,1,0:T(8,128)} fusion(bf16[8,128,2048,1]{2,1,3,0:T(8,128)(2,1)} %bitcast.143, bf16[8,4,2048,128]{2,3,1,0:T(8,128)(2,1)} %copy.40, pred[8,4]{1,0:T(8,128)(4,1)S(1)} %compare_and_fusion), kind=kOutput, calls=%fused_computation.2 | convolution fusion | flops 2155872256 | bytes 23068704 | tf_op jit(solution)/shard_map/rtd,drmc->rtmc/dot_general | solution.py:127
  75.7 4.7 %all-to-all-start = ((f32[4,2,128,4,128]{2,4,3,1,0:T(8,128)}), f32[4,2,128,4,128]{2,4,3,1,0:T(8,128)}, u32[]{:S(2)}, u32[]{:S(2)}) async-start(f32[4,2,128,4,128]{2,4,3,1,0:T(8,128)} %bitcast.125), calls=%async_computation | async-start | bytes 4194304 | tf_op jit(solution)/shard_map/all_to_all | solution.py:22
  80.6 24.3 %all-to-all-done = f32[4,2,128,4,128]{2,4,3,1,0:T(8,128)} async-done(((f32[4,2,128,4,128]{2,4,3,1,0:T(8,128)}), f32[4,2,128,4,128]{2,4,3,1,0:T(8,128)}, u32[]{:S(2)}, u32[]{:S(2)}) %all-to-all-start) | async-done | bytes 2097184 | tf_op jit(solution)/shard_map/all_to_all | solution.py:22
  104.9 1.8 reduce_sum.73
  106.9 2.5 fusion.8
  109.4 1.3 copy-done.2
  110.7 3.8 %fusion.12 = (f32[2,128]{1,0:T(2,128)S(1)}, f32[2,128]{1,0:T(2,128)S(1)}) fusion(f32[2,10,128,128]{3,1,2,0:T(8,128)S(1)} %get-tuple-element.64, f32[2,128]{1,0:T(2,128)S(1)} %get-tuple-element.63, pred[2,10]{1,0:T(4,128)(4,1)S(1)} %compare_reduce_fusion), kind=kLoop, calls=%fused_computation.18 | loop fusion | flops 1637888 | bytes 1313812 | tf_op jit(solution)/shard_map/reduce_sum | solution.py:150
  114.6 1.5 reduce_max.19
  116.2 2.8 %exponential_reduce_fusion = (f32[256]{0:T(256)S(1)}, f32[256]{0:T(256)S(1)}) fusion(f32[256,1280]{1,0:T(8,128)} %reduce-scatter.2.cloned.1.call-done, f32[256]{0:T(256)S(1)} %reduce_max.19, f32[256]{0:T(256)S(1)} %bitcast.126, f32[32,8,10,128]{3,2,1,0:T(8,128)} %bitcast.118, pred[32,8,10,128]{3,2,1,0:T(8,128)(4,1)S(1)} %bitcast.121), kind=kLoop, calls=%fused_computation.31 | loop fusion | flops 1965568 | bytes 2953216 | tf_op jit(solution)/shard_map/reduce_sum | solution.py:152
  119.1 32.2 %all_to_all.25 = f32[64,6,256]{2,1,0:T(8,128)S(1)} all-to-all(f32[64,6,256]{2,1,0:T(8,128)S(1)} %broadcast_in_dim.61), channel_id=1, replica_groups=mesh['seq'=4,'vocab_0'=4,'vocab_1'=8,'vocab_2'=2] {'vocab_0','vocab_1','..., dimensions={0} | all-to-all | bytes 786432 | tf_op jit(solution)/shard_map/all_to_all | solution.py:28
  151.3 0.3 fusion.46
  153.2 2.9 %fusion.25 = bf16[256,1280]{1,0:T(8,128)(2,1)S(1)} fusion(f32[256,1280]{1,0:T(8,128)} %reduce-scatter.2.cloned.1.call-done, f32[32,8,10,128]{3,2,1,0:T(8,128)} %bitcast.119, f32[256]{0:T(256)S(1)} %bitcast.131, f32[256]{0:T(256)S(1)} %bitcast.128, f32[256]{0:T(256)S(1)} %bitcast.133, f32[256]{0:T(256)S(1)} %bitcast.135, pred[32,8,10,128]{3,2,1,0:T(8,128)(4,1)S(1)} %bitcast.122), kind=kLoop, calls=%fused_computation.32 | loop fusion | flops 2621440 | bytes 3608576 | tf_op jit(solution)/shard_map/convert_element_type | solution.py:170
  156.3 34.2 %all_to_all.26 = bf16[4,256,1280]{2,1,0:T(8,128)(2,1)S(1)} all-to-all(bf16[4,256,1280]{2,1,0:T(8,128)(2,1)S(1)} %broadcast_in_dim.62), channel_id=1, replica_groups=mesh['seq'=4,'vocab_0'=4,'vocab_1'=8,'vocab_2'=2] {'seq'}, dimensions={0} | all-to-all | bytes 5242880 | tf_op jit(solution)/shard_map/all_to_all | solution.py:28
  190.5 1.5 copy-done.3
  192.0 2.9 %fusion.13 = f32[2,32,16,896]{3,2,0,1:T(8,128)S(1)} fusion(bf16[32,2,16,1280]{3,2,1,0:T(8,128)(2,1)S(1)} %bitcast.123, bf16[896,1280]{1,0:T(8,128)(2,1)S(1)} %copy-done), kind=kOutput, calls=%fused_computation.19 | convolution fusion | flops 2348810240 | bytes 8585216 | tf_op jit(solution)/shard_map/dot_general | solution.py:175
  194.9 0.3 copy.49
  195.2 8.5 %all_to_all.27 = f32[2,32,16,896]{3,2,1,0:T(8,128)} all-to-all(f32[2,32,16,896]{3,2,1,0:T(8,128)S(1)} %copy.49), channel_id=1, replica_groups=mesh['seq'=4,'vocab_0'=4,'vocab_1'=8,'vocab_2'=2] {'vocab_2'}, dimensions={0} | all-to-all | bytes 7340032 | tf_op jit(solution)/shard_map/all_to_all | solution.py:22
  203.7 3.7 %reduce_sum.78 = f32[32,16,896]{2,1,0:T(8,128)} reduce(f32[2,32,16,896]{3,2,1,0:T(8,128)} %all_to_all.27, f32[]{:T(128)} %constant.68.clone.1), dimensions={0}, to_apply=%region_10.11 | reduce | flops 458752 | bytes 5505028 | tf_op jit(solution)/shard_map/reduce_sum | solution.py:23
  207.4 5.3 %all-to-all-start.4 = ((f32[32,16,896]{2,1,0:T(8,128)}), f32[32,16,896]{2,1,0:T(8,128)}, u32[]{:S(2)}, u32[]{:S(2)}) async-start(f32[32,16,896]{2,1,0:T(8,128)} %reduce_sum.78), calls=%async_computation.5 | async-start | bytes 3670016 | tf_op jit(solution)/shard_map/all_to_all | solution.py:78
  212.7 0.6 subtract_subtract_fusion
  213.3 6.6 %fusion.5 = bf16[896,1280]{0,1:T(8,128)(2,1)} fusion(bf16[1024,1280]{1,0:T(8,128)(2,1)} %bitcast.124, bf16[1024,896]{1,0:T(8,128)(2,1)} %param.7), kind=kOutput, calls=%fused_computation.8 | convolution fusion | flops 2349957120 | bytes 6750208 | tf_op jit(solution)/shard_map/dot_general | solution.py:172
  219.9 4.2 %copy.50 = bf16[896,1280]{1,0:T(8,128)(2,1)} copy(bf16[896,1280]{0,1:T(8,128)(2,1)} %fusion.5) | data formatting | bytes 4587520
  224.0 31.7 %all-to-all-done.4 = f32[32,16,896]{2,1,0:T(8,128)} async-done(((f32[32,16,896]{2,1,0:T(8,128)}), f32[32,16,896]{2,1,0:T(8,128)}, u32[]{:S(2)}, u32[]{:S(2)}) %all-to-all-start.4) | async-done | bytes 1835040 | tf_op jit(solution)/shard_map/all_to_all | solution.py:78
  255.7 2.2 reduce_sum.79
  (109 shorter events, 3.1 us)
Async XLA Ops:
  7.2 1.7 copy-start
  7.2 107.4 %reduce-scatter.2.cloned.1.call-start = ((), (), s32[]{:S(2)}) async-start(), calls=%async_computation.6 | async-start | bytes 6553600 | tf_op jit(solution)/shard_map/reduce_scatter | solution.py:140
  15.6 0.7 copy-start.1
  75.7 29.2 %all-to-all-start = ((f32[4,2,128,4,128]{2,4,3,1,0:T(8,128)}), f32[4,2,128,4,128]{2,4,3,1,0:T(8,128)}, u32[]{:S(2)}, u32[]{:S(2)}) async-start(f32[4,2,128,4,128]{2,4,3,1,0:T(8,128)} %bitcast.125), calls=%async_computation | async-start | bytes 4194304 | tf_op jit(solution)/shard_map/all_to_all | solution.py:22
  109.4 1.3 copy-start.2
  190.5 1.5 copy-start.3
  207.4 48.3 %all-to-all-start.4 = ((f32[32,16,896]{2,1,0:T(8,128)}), f32[32,16,896]{2,1,0:T(8,128)}, u32[]{:S(2)}, u32[]{:S(2)}) async-start(f32[32,16,896]{2,1,0:T(8,128)} %reduce_sum.78), calls=%async_computation.5 | async-start | bytes 3670016 | tf_op jit(solution)/shard_map/all_to_all | solution.py:78
Sparse Core Ops, SparseCore 0:
  15.7 61.7 reduce-scatter.1
where the time goes:
time: 267 us; the launch traced here: 265 us
  blocking collectives  74.9 us (28%)
  local copies, waits for them, and re-layouts  60.1 us (23%)
  waiting for transfers between devices  56 us (21%)
  matrix products  29.3 us (11%)
  other arithmetic  20.1 us (8%)
  between operations  14.4 us (5%)
  starting transfers between devices  10 us (4%)
    all_to_all x2, blocking collectives, sent_to_all(): lax.all_to_all(jnp.broadcast_to(array[None], (devices, *array.shape)), ax...  66.4 us
    all_to_all x1, waiting for transfers between devices, sum_by_axis(): lax.all_to_all(nearer, far, split_axis=0, concat_axis=0, tiled=True)  31.7 us
    gather x2, local copies, waits for them, and re-layouts, body(): picked = jnp.take(head_blocks, safe_ids, axis=1)  31.4 us
    all_to_all x1, waiting for transfers between devices, sent_and_summed(): lax.all_to_all(tiles, axis, split_axis=0, concat_axis=0, tiled=True)  24.3 us
    unnamed x11, local copies, waits for them, and re-layouts  17.2 us
    dot_general x1, matrix products, body(): jnp.einsum('rtd,drmc->rtmc', hidden_blocks, picked, preferred_element_typ...  10.6 us
    all_to_all x1, blocking collectives, sent_and_summed(): lax.all_to_all(tiles, axis, split_axis=0, concat_axis=0, tiled=True)  8.48 us
    reshape x1, local copies, waits for them, and re-layouts, body(): head_blocks = teacher_head.reshape(teacher_part, blocks_dev, BLOCK)  8.11 us
  transfers between devices with their start and end apart: 3, of which 2 were waited for; matrix products, arithmetic and copies ran while one was open for 30% of the time, Pallas kernels for 0%

commit v1 on v0

v1 whole, which is shorter than its diff:
```python
import functools

import jax
import jax.numpy as jnp
from jax import lax
from jax.experimental import pallas as pl
from jax.experimental.pallas import tpu as pltpu
from jax.sharding import Mesh
from jax.sharding import PartitionSpec as P

VOCAB = ("y", "z", "c")
BLOCK = 128
MOST = 4
GROUP = 16
ROW_BLOCKS = 8
SLOTS = ROW_BLOCKS * MOST
STATS = 5
HALF_ROWS = ROW_BLOCKS * GROUP

masked_value = -1e30
loss_scale = 2048.0
f32 = jnp.float32
bf16 = jnp.bfloat16
MIB = 1024 * 1024


def whole(shape):
    return pl.BlockSpec(shape, lambda i: (0,) * len(shape))


def call(kernel, scalars, arrays, outs, scratch=(), limit=52):
    return pl.pallas_call(
        kernel,
        grid=(1,),
        in_specs=[pl.BlockSpec(memory_space=pltpu.SMEM)] * len(scalars)
        + [whole(array.shape) for array in arrays],
        out_specs=[whole(shape) for shape, _ in outs],
        out_shape=[jax.ShapeDtypeStruct(shape, dtype) for shape, dtype in outs],
        scratch_shapes=list(scratch),
        compiler_params=pltpu.CompilerParams(vmem_limit_bytes=limit * MIB),
    )(*scalars, *arrays)


def group_rows(row_block, owner, half):
    return pl.ds(pl.multiple_of(row_block * BLOCK + owner * 32 + half * GROUP, GROUP), GROUP)


def teacher_slots(owners, ids, valid, hidden, head, lhs, store):
    def row_block(r, carry):
        for place in range(4):
            rows = pl.ds(pl.multiple_of(r * BLOCK + owners[place] * 32, 32), 32)
            lhs[place * 32 : (place + 1) * 32, :] = hidden[rows, :]
        rows = pl.ds(pl.multiple_of(r * GROUP, GROUP), GROUP)
        for m in range(MOST):
            slot = r * MOST + m

            @pl.when(valid[slot] > 0)
            def _():
                cols = pl.ds(pl.multiple_of(ids[slot] * BLOCK, BLOCK), BLOCK)
                part = jnp.dot(lhs[...], head[:, cols], preferred_element_type=f32)
                for place in range(4):
                    store(rows, m, place, part[place * 32 : (place + 1) * 32])

        return carry

    lax.fori_loop(0, ROW_BLOCKS, row_block, 0)


def gather_rows(owners, hidden, lhs):
    for half in range(2):
        for place in range(4):
            for r in range(ROW_BLOCKS):
                low = (half * 4 + place) * HALF_ROWS + r * GROUP
                lhs[low : low + GROUP, :] = hidden[group_rows(r, owners[place], half), :]


def student_kernel(owners, hidden, head, far_l, far_r, nxt0, prv0, own0, nxt1, prv1, own1, lhs):
    gather_rows(owners, hidden, lhs)
    width = far_l.shape[2]
    for half, wide in enumerate(((nxt0, prv0, own0), (nxt1, prv1, own1))):
        rows = slice(half * 4 * HALF_ROWS, (half + 1) * 4 * HALF_ROWS)
        for side, far in enumerate((far_l, far_r)):
            cols = slice(side * width, (side + 1) * width)
            part = jnp.dot(lhs[rows], head[:, cols], preferred_element_type=f32)
            far[half] = part[:HALF_ROWS]
            for place, ref in enumerate(wide):
                ref[:, cols] = part[(place + 1) * HALF_ROWS : (place + 2) * HALF_ROWS]


def student_partial(owners, hidden, head):
    cols = head.shape[1]
    return call(
        student_kernel,
        [owners],
        [hidden, head],
        [((2, HALF_ROWS, cols // 2), f32)] * 2 + [((HALF_ROWS, cols), f32)] * 6,
        [pltpu.VMEM(hidden.shape, bf16)],
    )


def teacher_kernel(owners, ids, valid, hidden, head, far_l, far_r, nxt, prv, own, lhs):
    wide = (nxt, prv, own)
    for ref in (far_l, far_r, *wide):
        ref[...] = jnp.zeros(ref.shape, f32)

    def store(rows, m, place, part):
        for half in range(2):
            value = part[half * GROUP : (half + 1) * GROUP]
            if place == 0:
                low = (m % 2) * BLOCK
                (far_l, far_r)[m // 2][half, rows, low : low + BLOCK] = value
            else:
                wide[place - 1][half, rows, m * BLOCK : (m + 1) * BLOCK] = value

    teacher_slots(owners, ids, valid, hidden, head, lhs, store)


def teacher_partial(owners, ids, valid, hidden, head):
    return call(
        teacher_kernel,
        [owners, ids, valid],
        [hidden, head],
        [((2, HALF_ROWS, 2 * BLOCK), f32)] * 2 + [((2, HALF_ROWS, MOST * BLOCK), f32)] * 3,
        [pltpu.VMEM((BLOCK, head.shape[0]), bf16)],
    )


def student_merge_kernel(half, nxt, prv, from_prev, from_next, to_next, to_prev):
    cut = from_prev.shape[2]
    to_next[:, :cut] = nxt[:, :cut] + from_prev[half]
    to_next[:, cut:] = nxt[:, cut:]
    to_prev[:, :cut] = prv[:, :cut]
    to_prev[:, cut:] = prv[:, cut:] + from_next[half]


def teacher_merge_kernel(nxt, prv, from_prev, from_next, to_next, to_prev):
    cut = from_prev.shape[2]
    to_next[:, :, :cut] = nxt[:, :, :cut] + from_prev[...]
    to_next[:, :, cut:] = nxt[:, :, cut:]
    to_prev[:, :, :cut] = prv[:, :, :cut]
    to_prev[:, :, cut:] = prv[:, :, cut:] + from_next[...]


def merge(kernel, *parts):
    return call(kernel, [], parts, [(parts[0].shape, f32)] * 2)


def turn_kernel(owners, core, hidden, head, turned_hidden, turned_head, lhs):
    gather_rows(owners, hidden, lhs)
    turned_hidden[...] = lhs[...].T
    for part in range(2):
        rows = pl.ds(pl.multiple_of(core[part] * 384, 128), 512)
        turned_head[part] = head[rows, :].T


def turned(owners, core, hidden, head):
    return call(
        turn_kernel,
        [owners, core],
        [hidden, head],
        [((hidden.shape[1], hidden.shape[0]), bf16), ((2, head.shape[1], 512), bf16)],
        [pltpu.VMEM(hidden.shape, bf16)],
    )


def stats_kernel(half, ids, valid, own, from_prev, from_next, town, tprev, tnext, first, e_out, w_out, stats, logits, tile):
    lane = lax.broadcasted_iota(jnp.int32, (GROUP, BLOCK), 1)
    for r in range(ROW_BLOCKS):
        rows = slice(r * GROUP, (r + 1) * GROUP)
        student = own[rows] + from_prev[rows] + from_next[rows]
        logits[rows] = student
        student_top = jnp.max(student, axis=1, keepdims=True)
        student_exp = jnp.exp(student - student_top)
        e_out[rows] = student_exp
        student_total = jnp.sum(student_exp, axis=1, keepdims=True)
        teacher = []
        for m in range(MOST):
            cols = slice(m * BLOCK, (m + 1) * BLOCK)
            value = town[half, rows, cols] + tprev[half, rows, cols] + tnext[half, rows, cols]
            teacher.append(jnp.where(valid[r * MOST + m] > 0, value, masked_value))
        highest = functools.reduce(jnp.maximum, teacher)
        teacher_top = jnp.max(highest, axis=1, keepdims=True)
        total = gap = jnp.zeros((GROUP, BLOCK), f32)
        for m in range(MOST):
            slot = r * MOST + m
            weight = jnp.where(valid[slot] > 0, jnp.exp(teacher[m] - teacher_top), 0.0)
            w_out[slot] = weight
            cols = pl.ds(pl.multiple_of(ids[slot] * BLOCK, BLOCK), BLOCK)
            total += weight
            gap += weight * (teacher[m] - logits[rows, cols])
        columns = (
            teacher_top,
            jnp.sum(total, axis=1, keepdims=True),
            jnp.sum(gap, axis=1, keepdims=True),
            student_top,
            student_total,
        )
        line = jnp.zeros((GROUP, BLOCK), f32)
        for k, column in enumerate(columns):
            line = jnp.where(lane == k, column, line)
        tile[rows] = line
    if half == 0:
        stats[...] = tile[...].T[:8]
    else:
        both = (first[...], tile[...].T[:8])
        lines = [jnp.concatenate([part[k : k + 1] for k in range(STATS)], axis=1) for part in both]
        stats[...] = jnp.broadcast_to(jnp.concatenate(lines, axis=0)[None], stats.shape)


def local_stats(half, ids, valid, student, teacher, first, sent):
    cols = student[0].shape[1]
    return call(
        functools.partial(stats_kernel, half),
        [ids, valid],
        [*student, *teacher, first],
        [((HALF_ROWS, cols), f32), ((SLOTS, GROUP, BLOCK), f32), (sent, f32)],
        [pltpu.VMEM((HALF_ROWS, cols), f32), pltpu.VMEM((HALF_ROWS, BLOCK), f32)],
    )


def grad_kernel(half, ids, e_in, w_in, mine, merged, grad, loss, work):
    def stat(k):
        return merged[:, half, k * BLOCK : (k + 1) * BLOCK]

    def own_stat(k):
        return mine[0, half : half + 1, k * BLOCK : (k + 1) * BLOCK]

    teacher_top = jnp.max(stat(0), axis=0, keepdims=True)
    teacher_scale = jnp.exp(stat(0) - teacher_top)
    teacher_total = jnp.sum(stat(1) * teacher_scale, axis=0, keepdims=True)
    gap = jnp.sum(stat(2) * teacher_scale, axis=0, keepdims=True)
    student_top = jnp.max(stat(3), axis=0, keepdims=True)
    student_total = jnp.sum(stat(4) * jnp.exp(stat(3) - student_top), axis=0, keepdims=True)
    loss_row = (gap / teacher_total - teacher_top - jnp.log(teacher_total)) + (
        student_top + jnp.log(student_total)
    )
    loss[...] = jnp.broadcast_to(loss_row, loss.shape)
    student_factor = loss_scale * jnp.exp(own_stat(3) - student_top) / student_total
    teacher_factor = loss_scale * jnp.exp(own_stat(0) - teacher_top) / teacher_total
    line = lax.broadcasted_iota(jnp.int32, (HALF_ROWS, BLOCK), 0)
    factors = jnp.where(line == 0, student_factor, jnp.where(line == 1, teacher_factor, 0.0)).T
    work[...] = e_in[...] * factors[:, 0:1]
    for r in range(ROW_BLOCKS):
        rows = slice(r * GROUP, (r + 1) * GROUP)
        factor = factors[rows, 1:2]
        for m in range(MOST):
            slot = r * MOST + m
            cols = pl.ds(pl.multiple_of(ids[slot] * BLOCK, BLOCK), BLOCK)
            work[rows, cols] = work[rows, cols] - factor * w_in[slot]
    grad[...] = work[...].astype(bf16)


def logit_grads(half, ids, e_in, w_in, mine, merged):
    return call(
        functools.partial(grad_kernel, half),
        [ids],
        [e_in, w_in, mine, merged],
        [(e_in.shape, bf16), ((8, BLOCK), f32)],
        [pltpu.VMEM(e_in.shape, f32)],
    )


def hidden_kernel(owners, far, after, before, own, turned_head, keep, give, rows, work):
    for place, piece in enumerate((far, after, before, own)):
        rows[place * HALF_ROWS : (place + 1) * HALF_ROWS, :] = piece[...]
    for part, out in ((1, give), (0, keep)):
        work[...] = jnp.dot(rows[...], turned_head[part], preferred_element_type=f32)
        for place in range(4):
            zl = owners[place]
            for y in range(4):
                for zh in range(2):
                    low = place * HALF_ROWS + y * 32 + zh * GROUP
                    out[y, zh * 4 + zl] = work[low : low + GROUP, :]


def hidden_partial(owners, pieces, turned_head):
    width = turned_head.shape[2]
    return call(
        hidden_kernel,
        [owners],
        [*pieces, turned_head],
        [((4, 8, GROUP, width), f32)] * 2,
        [pltpu.VMEM((4 * HALF_ROWS, pieces[0].shape[1]), bf16), pltpu.VMEM((4 * HALF_ROWS, width), f32)],
    )


def head_kernel(turned_hidden, *refs):
    pieces = refs[:8]
    out, grads = refs[8:]
    for k in range(8):
        grads[k * HALF_ROWS : (k + 1) * HALF_ROWS, :] = pieces[k][...]
    step = 256
    for low in range(0, out.shape[1], step):
        cols = slice(low, low + step)
        out[:, cols] = jnp.dot(turned_hidden[...], grads[:, cols], preferred_element_type=f32).astype(bf16)


def head_total(turned_hidden, pieces):
    depth, tokens = turned_hidden.shape
    cols = pieces[0].shape[1]
    return call(
        head_kernel,
        [],
        [turned_hidden, *pieces],
        [((depth, cols), bf16)],
        [pltpu.VMEM((tokens, cols), bf16)],
    )[0]


def after(earlier, arrays):
    return lax.optimization_barrier((earlier, arrays))[1]


def shift(array, axis, step):
    size = lax.axis_size(axis)
    return lax.ppermute(array, axis, [(k, (k + step) % size) for k in range(size)])


def slots_of(kept, first, blocks):
    before = jnp.sum((kept < first).astype(jnp.int32), axis=1)
    place = jnp.arange(kept.shape[1], dtype=jnp.int32)
    wanted = before[:, None] + jnp.arange(MOST, dtype=jnp.int32)[None, :]
    chosen = (place[None, None, :] == wanted[:, :, None]) & (kept < first + blocks)[:, None, :]
    ids = jnp.sum(jnp.where(chosen, kept[:, None, :] - first, 0), axis=2)
    valid = jnp.any(chosen, axis=2)
    return ids.reshape(-1), valid.astype(jnp.int32).reshape(-1)


def body(teacher_hidden, teacher_head, student_hidden, student_head, kept):
    blocks = teacher_head.shape[1] // BLOCK
    x, c = lax.axis_index("x"), lax.axis_index("c")
    around = jnp.array([2, 1, 3, 0], jnp.int32)
    owners = ((x + around) % 4).astype(jnp.int32)
    core = jnp.stack([c, 1 - c]).astype(jnp.int32)
    ids, valid = slots_of(kept, lax.axis_index(VOCAB) * blocks, blocks)

    def to_both(to_next, to_prev):
        return shift(to_next, "x", 1), shift(to_prev, "x", -1)

    far_l, far_r, nxt0, prv0, own0, nxt1, prv1, own1 = student_partial(
        owners, student_hidden, student_head
    )
    tfar_l, tfar_r, tnxt, tprv, town = teacher_partial(
        owners, ids, valid, *after(own1, (teacher_hidden, teacher_head))
    )
    far, tfar = to_both(far_l, far_r), to_both(tfar_l, tfar_r)
    merged0 = merge(functools.partial(student_merge_kernel, 0), *after(town, (nxt0, prv0)), *far)
    tmerged = merge(teacher_merge_kernel, *after(merged0[0], (tnxt, tprv)), *tfar)
    merged1 = merge(
        functools.partial(student_merge_kernel, 1), *after(tmerged[0], (nxt1, prv1)), *far
    )
    logits0 = (own0, *to_both(*merged0))
    teacher = (town, *to_both(*tmerged))
    logits1 = (own1, *to_both(*merged1))
    turned_hidden, turned_head = turned(owners, core, *after(merged1[0], (student_hidden, student_head)))

    def spread(grad):
        return shift(grad, "x", 2), shift(grad, "x", -1), shift(grad, "x", 1), grad

    def row_sums(pieces):
        keep, give = hidden_partial(owners, pieces, turned_head)
        return keep, shift(give, "c", 1)

    devices = lax.axis_size(VOCAB)
    nothing = jnp.zeros((8, BLOCK), f32)
    e0, w0, first = local_stats(
        0, ids, valid, after(turned_head, logits0), teacher, nothing, (8, BLOCK)
    )
    e1, w1, mine = local_stats(1, ids, valid, logits1, teacher, first, (devices, 2, STATS * BLOCK))
    every = lax.all_to_all(mine, VOCAB, 0, 0, tiled=True)
    grad0, loss0 = logit_grads(0, ids, e0, w0, mine, every)
    grad1, loss1 = logit_grads(1, ids, e1, w1, mine, after(grad0, every))
    pieces0, pieces1 = after(grad1, spread(grad0)), spread(grad1)
    keep0, got0 = row_sums(pieces0)
    over_y0 = lax.all_to_all(keep0 + got0, "y", 0, 0, tiled=True)
    rows0 = over_y0.sum(axis=0)
    pieces1 = after(rows0, pieces1)
    keep1, got1 = row_sums(pieces1)
    over_y1 = lax.all_to_all(keep1 + got1, "y", 0, 0, tiled=True)
    loss = jnp.concatenate([loss0, loss1], axis=1)
    losses = [loss] + [shift(loss, "x", step) for step in (1, 2, 3)]
    head_grad = head_total(turned_hidden, (*pieces0, *pieces1))
    (head_grad, losses), over_y1 = lax.optimization_barrier(((head_grad, losses), over_y1))
    both = jnp.concatenate([rows0, over_y1.sum(axis=0)], axis=1)
    both = lax.all_to_all(both, "z", 0, 0, tiled=True)
    both = both.sum(axis=0).astype(bf16)
    sum0, sum1 = both[:GROUP], both[GROUP:]
    keep = jnp.where(c == 0, sum0, sum1)
    got = shift(jnp.where(c == 0, sum1, sum0), "c", 1)
    low, high = jnp.where(c == 0, keep, got), jnp.where(c == 0, got, keep)
    hidden_grad = jnp.concatenate([low, high[:, BLOCK:]], axis=1)

    row = jnp.stack([part[0] for part in losses]).reshape(4, 2, 4, 2, GROUP)
    row = lax.dynamic_index_in_dim(row, x, 2, keepdims=False)
    row = jnp.take(row, (x - jnp.arange(4)) % 4, axis=0)
    loss_rows = row.transpose(2, 0, 1, 3).reshape(-1)
    return loss_rows, hidden_grad, head_grad


def solution(mesh):
    split = Mesh(mesh.devices.reshape(4, 4, 8, 2), ("x", "y", "z", "c"))
    in_specs = (P(None, "x"), P("x", VOCAB), P(None, "x"), P("x", VOCAB), P())
    out_specs = (P("x"), P(VOCAB, "x"), P("x", VOCAB))
    return jax.shard_map(body, mesh=split, in_specs=in_specs, out_specs=out_specs, check_vma=False)
```

time: 267 us -> 222 us (0.83)
  local copies, waits for them, and re-layouts: 60.1 us -> 6.24 us
  Pallas kernels: 0 us -> 48.5 us
  blocking collectives: 74.9 us -> 31.5 us
  waiting for transfers between devices: 56 us -> 86.3 us
  matrix products: 29.3 us -> 0 us
  starting transfers between devices: 10 us -> 38.1 us
  between operations: 14.4 us -> 0.84 us
  other arithmetic: 20.1 us -> 9.25 us
    ppermute x0 -> x22, waiting for transfers between devices: none -> 53.5 us  [shift(): lax.ppermute(array, axis, [(k, (k + step) % size) for k in range(size)])]
    pallas_call x0 -> x13, Pallas kernels: none -> 48.5 us  [call(): pl.pallas_call(kernel, grid=(1,), in_specs=[pl.BlockSpec(memory_space=plt...]
    all_to_all x3 -> x1, blocking collectives: 74.9 us -> 31.5 us  [body(): every = lax.all_to_all(mine, VOCAB, 0, 0, tiled=True)]
    gather x6 -> x1, local copies, waits for them, and re-layouts: 32.3 us -> 0.57 us  [body(): row = jnp.take(row, (x - jnp.arange(4)) % 4, axis=0)]
    dot_general x5 -> x0, matrix products: 29.3 us -> none  [the longest x1 10.6 us: body(): jnp.einsum('rtd,drmc->rtmc', hidden_blocks, picked, preferred_element_typ...]
    ppermute x0 -> x22, starting transfers between devices: none -> 25.8 us  [shift(): lax.ppermute(array, axis, [(k, (k + step) % size) for k in range(size)])]
    all_to_all x2 -> x3, waiting for transfers between devices: 56 us -> 32.9 us  [the longest x1 15.1 us: body(): both = lax.all_to_all(both, 'z', 0, 0, tiled=True)]
    reduce_sum x6 -> x5, other arithmetic: 14.4 us -> 1.79 us  [the longest x1 1.33 us: body(): rows0 = over_y0.sum(axis=0)]
  transfers between devices with their start and end apart: 3 -> 25, of which waited for: 2 -> 16; matrix products, arithmetic and copies ran while one was open for 30% -> 2% of each run, Pallas kernels for 0% -> 12%
where the time goes in v1:
time: 222 us; the launch traced here: 221 us
  waiting for transfers between devices  86.3 us (39%)
  Pallas kernels  48.5 us (22%)
  starting transfers between devices  38.1 us (17%)
  blocking collectives  31.5 us (14%)
  other arithmetic  9.25 us (4%)
  local copies, waits for them, and re-layouts  6.24 us (3%)
    ppermute x22, waiting for transfers between devices, shift(): lax.ppermute(array, axis, [(k, (k + step) % size) for k in range(size)])  53.5 us
    pallas_call x13, Pallas kernels, call(): pl.pallas_call(kernel, grid=(1,), in_specs=[pl.BlockSpec(memory_space=plt...  48.5 us
    all_to_all x1, blocking collectives, body(): every = lax.all_to_all(mine, VOCAB, 0, 0, tiled=True)  31.5 us
    ppermute x22, starting transfers between devices, shift(): lax.ppermute(array, axis, [(k, (k + step) % size) for k in range(size)])  25.8 us
    all_to_all x1, waiting for transfers between devices, body(): both = lax.all_to_all(both, 'z', 0, 0, tiled=True)  15.1 us
    all_to_all x1, waiting for transfers between devices, body(): over_y0 = lax.all_to_all(keep0 + got0, 'y', 0, 0, tiled=True)  12.1 us
    all_to_all x1, waiting for transfers between devices, body(): over_y1 = lax.all_to_all(keep1 + got1, 'y', 0, 0, tiled=True)  5.67 us
    unnamed x29, local copies, waits for them, and re-layouts  4.55 us
  transfers between devices with their start and end apart: 25, of which 16 were waited for; matrix products, arithmetic and copies ran while one was open for 2% of the time, Pallas kernels for 12%

profile of v1, /device:TPU:1, one launch (start us, length us, event | category | flops | bytes accessed | tf_op | source)
XLA Modules:
  0.0 220.8 jit_solution(18312567852047760462)
XLA Ops:
  1.3 6.7 %shard_map.85 = (f32[2,128,640]{2,1,0:T(8,128)S(1)}, f32[2,128,640]{2,1,0:T(8,128)S(1)}, f32[128,1280]{1,0:T(8,128)S(1)}, f32[128,1280]{1,0:T(8,128)}, f32[128,1...) custom-call(s32[4]{0:T(128)S(1)} %and_select_fusion.1.owners, ...), custom_call_target="tpu_custom_call" | custom-call | tf_op jit(solution)/shard_map/pallas_call | solution.py:32
  8.1 2.0 collective-permute-start
  12.3 8.2 %shard_map.86 = (f32[2,128,256]{2,1,0:T(8,128)S(1)}, f32[2,128,256]{2,1,0:T(8,128)S(1)}, f32[2,128,512]{2,1,0:T(8,128)S(1)}, f32[2,128,512]{2,1,0:T(8,128)S(1)}, f32[2,128,512]{2,1,0:T(8,128)}) custom-call(s32[4]{0:T(128)S(1)} %and_select_fusion.1.owners, s32[32]{0:T(128)S(1)} %reshape.97.ids, s32[32]{0:T(128)S(1)} %reshape.100.valid, ...), custom_call_target="tpu_custom_call" | custom-call | tf_op jit(solution)/shard_map/pallas_call | solution.py:32
  23.5 1.6 collective-permute-done.1.from_next
  26.0 1.6 shard_map.87
  31.9 16.1 %collective-permute-done.2.from_prev = f32[2,128,256]{2,1,0:T(8,128)S(1)} collective-permute-done((f32[2,128,256]{2,1,0:T(8,128)S(1)}, f32[2,128,256]{2,1,0:T(8,128)S(1)}, u32[]{:S(2)}, u32[]{:S(2)}) %collective-permute-start.2) | collective-permute-done | bytes 262176 | tf_op jit(solution)/shard_map/ppermute | solution.py:316
  48.0 2.2 %shard_map.88 = (f32[2,128,512]{2,1,0:T(8,128)}, f32[2,128,512]{2,1,0:T(8,128)}) custom-call(f32[2,128,512]{2,1,0:T(8,128)} %copy-done.8, f32[2,128,512]{2,1,0:T(8,128)} %copy-done.9, f32[2,128,256]{2,1,0:T(8,128)S(1)} %collective-permute-done.2.from_prev, f32[2,128,256]{2,1,0:T(8,128)S(1)} %collective-permute-done.3.from_next), custom_call_target="tpu_custom_call" | custom-call | tf_op jit(solution)/shard_map/pallas_call | solution.py:32
  50.2 2.4 %shard_map.89 = (f32[128,1280]{1,0:T(8,128)}, f32[128,1280]{1,0:T(8,128)S(1)}) custom-call(f32[128,1280]{1,0:T(8,128)S(1)} %copy-done.5, f32[128,1280]{1,0:T(8,128)} %get-tuple-element.87.prv, f32[2,128,640]{2,1,0:T(8,128)} %copy-done.10, f32[2,128,640]{2,1,0:T(8,128)} %copy-done.11), custom_call_target="tpu_custom_call" | custom-call | tf_op jit(solution)/shard_map/pallas_call | solution.py:32
  56.1 2.6 %collective-permute-start.7 = (f32[2,128,512]{2,1,0:T(8,128)}, f32[2,128,512]{2,1,0:T(8,128)S(1)}, u32[]{:S(2)}, u32[]{:S(2)}) collective-permute-start(f32[2,128,512]{2,1,0:T(8,128)} %get-tuple-element.93), channel_id=1, source_target_pairs={{0,192},{64,0},{128,64},{192,128},{1,193},{65,1},{129,65},{193,129... | collective-permute-start | bytes 1572872 | tf_op jit(solution)/shard_map/ppermute | solution.py:316
  58.9 5.0 %shard_map.90 = (bf16[896,1024]{1,0:T(8,128)(2,1)S(1)}, bf16[2,1280,512]{2,1,0:T(8,128)(2,1)}) custom-call(s32[4]{0:T(128)S(1)} %and_select_fusion.1.owners, s32[2]{0:T(128)S(1)} %pad_add_fusion.core, bf16[1024,896]{1,0:T(8,128)(2,1)} %hidden.3, bf16[896,1280]{1,0:T(8,128)(2,1)} %head.3), custom_call_target="tpu_custom_call" | custom-call | tf_op jit(solution)/shard_map/pallas_call | solution.py:32
  65.1 12.7 %collective-permute-done.6.tprev = f32[2,128,512]{2,1,0:T(8,128)S(1)} collective-permute-done((f32[2,128,512]{2,1,0:T(8,128)}, f32[2,128,512]{2,1,0:T(8,128)S(1)}, u32[]{:S(2)}, u32[]{:S(2)}) %collective-permute-start.6) | collective-permute-done | bytes 524320 | tf_op jit(solution)/shard_map/ppermute | solution.py:316
  78.3 2.9 %shard_map.91 = (f32[128,1280]{1,0:T(8,128)}, f32[32,16,128]{2,1,0:T(8,128)S(1)}, f32[8,128]{1,0:T(8,128)S(1)}) custom-call(s32[32]{0:T(128)S(1)} %reshape.97.ids, s32[32]{0:T(128)S(1)} %reshape.100.valid, f32[128,1280]{1,0:T(8,128)} %get-tuple-element.97.own, f32[128,1280]{1,0:T(8,128)} %copy-done.12, f32[128,1280]{1,0:T(8,128)} %collective-permute-done.9.from_next, ...), custom_call_target="tpu_custom_call" | custom-call | tf_op jit(solution)/shard_map/pallas_call | solution.py:32
  81.3 2.9 %shard_map.92 = (f32[128,1280]{1,0:T(8,128)}, f32[32,16,128]{2,1,0:T(8,128)S(1)}, f32[64,2,640]{2,1,0:T(2,128)S(1)}) custom-call(s32[32]{0:T(128)S(1)} %reshape.97.ids, s32[32]{0:T(128)S(1)} %reshape.100.valid, f32[128,1280]{1,0:T(8,128)} %get-tuple-element.66.own, f32[128,1280]{1,0:T(8,128)} %collective-permute-done.4.from_prev, ...), custom_call_target="tpu_custom_call" | custom-call | tf_op jit(solution)/shard_map/pallas_call | solution.py:32
  84.2 31.5 %all_to_all.20.merged = f32[64,2,640]{2,1,0:T(2,128)S(1)} all-to-all(f32[64,2,640]{2,1,0:T(2,128)S(1)} %get-tuple-element.103.mine), channel_id=1, replica_groups=mesh['x'=4,'y'=4,'z'=8,'c'=2] {'y','z','c'}, dimensions={0} | all-to-all | bytes 655360 | tf_op jit(solution)/shard_map/all_to_all | solution.py:370
  117.8 1.6 collective-permute-start.11
  121.0 6.3 %collective-permute-done.10.far.refs_0_ = bf16[128,1280]{1,0:T(8,128)(2,1)S(1)} collective-permute-done((bf16[128,1280]{1,0:T(8,128)(2,1)S(1)}, bf16[128,1280]{1,0:T(8,128)(2,1)S(1)}, u32[]{:S(2)}, u32[]{:S(2)}) %collective-permute-start.10) | collective-permute-done | bytes 327712 | tf_op jit(solution)/shard_map/ppermute | solution.py:316
  127.3 7.1 %collective-permute-done.11.after.refs_1_ = bf16[128,1280]{1,0:T(8,128)(2,1)S(1)} collective-permute-done((bf16[128,1280]{1,0:T(8,128)(2,1)S(1)}, bf16[128,1280]{1,0:T(8,128)(2,1)S(1)}, u32[]{:S(2)}, u32[]{:S(2)}) %collective-permute-start.11) | collective-permute-done | bytes 327712 | tf_op jit(solution)/shard_map/ppermute | solution.py:316
  135.0 4.3 %shard_map.95 = (f32[4,8,16,512]{3,2,1,0:T(8,128)}, f32[4,8,16,512]{3,2,1,0:T(8,128)}) custom-call(s32[4]{0:T(128)S(1)} %and_select_fusion.1.owners, bf16[128,1280]{1,0:T(8,128)(2,1)S(1)} %collective-permute-done.10.far.refs_0_, bf16[128,1280]{1,0:T(8,128)(2,1)S(1)} %collective-permute-done.11.after.refs_1_, ...), custom_call_target="tpu_custom_call" | custom-call | tf_op jit(solution)/shard_map/pallas_call | solution.py:32
  139.9 2.5 %collective-permute-done.13 = f32[4,8,16,512]{3,2,1,0:T(8,128)S(1)} collective-permute-done((f32[4,8,16,512]{3,2,1,0:T(8,128)}, f32[4,8,16,512]{3,2,1,0:T(8,128)S(1)}, u32[]{:S(2)}, u32[]{:S(2)}) %collective-permute-start.13) | collective-permute-done | bytes 1048608 | tf_op jit(solution)/shard_map/ppermute | solution.py:316
  142.4 2.4 %add.86 = f32[4,8,16,512]{3,2,1,0:T(8,128)} add(f32[4,8,16,512]{3,2,1,0:T(8,128)} %get-tuple-element.113, f32[4,8,16,512]{3,2,1,0:T(8,128)S(1)} %collective-permute-done.13) | non-fusion elementwise | flops 262144 | bytes 3145728 | tf_op jit(solution)/shard_map/add | solution.py:375
  144.9 4.3 %all-to-all-start.1 = ((f32[4,8,16,512]{3,2,1,0:T(8,128)}), f32[4,8,16,512]{3,2,1,0:T(8,128)}, u32[]{:S(2)}, u32[]{:S(2)}) async-start(f32[4,8,16,512]{3,2,1,0:T(8,128)} %add.86), calls=%async_computation.1 | async-start | bytes 2097152 | tf_op jit(solution)/shard_map/all_to_all | solution.py:375
  151.9 12.1 %all-to-all-done.1 = f32[4,8,16,512]{3,2,1,0:T(8,128)} async-done(((f32[4,8,16,512]{3,2,1,0:T(8,128)}), f32[4,8,16,512]{3,2,1,0:T(8,128)}, u32[]{:S(2)}, u32[]{:S(2)}) %all-to-all-start.1) | async-done | bytes 1048608 | tf_op jit(solution)/shard_map/all_to_all | solution.py:375
  167.4 4.4 %shard_map.97 = (f32[4,8,16,512]{3,2,1,0:T(8,128)}, f32[4,8,16,512]{3,2,1,0:T(8,128)}) custom-call(s32[4]{0:T(128)S(1)} %and_select_fusion.1.owners, bf16[128,1280]{1,0:T(8,128)(2,1)S(1)} %collective-permute-done.14.refs_4_.far, bf16[128,1280]{1,0:T(8,128)(2,1)S(1)} %collective-permute-done.15.refs_5_.after, ...), custom_call_target="tpu_custom_call" | custom-call | tf_op jit(solution)/shard_map/pallas_call | solution.py:32
  172.3 2.5 %collective-permute-done.20 = f32[4,8,16,512]{3,2,1,0:T(8,128)S(1)} collective-permute-done((f32[4,8,16,512]{3,2,1,0:T(8,128)}, f32[4,8,16,512]{3,2,1,0:T(8,128)S(1)}, u32[]{:S(2)}, u32[]{:S(2)}) %collective-permute-start.20) | collective-permute-done | bytes 1048608 | tf_op jit(solution)/shard_map/ppermute | solution.py:316
  174.8 2.4 %add.87 = f32[4,8,16,512]{3,2,1,0:T(8,128)} add(f32[4,8,16,512]{3,2,1,0:T(8,128)} %get-tuple-element.121, f32[4,8,16,512]{3,2,1,0:T(8,128)S(1)} %collective-permute-done.20) | non-fusion elementwise | flops 262144 | bytes 3145728 | tf_op jit(solution)/shard_map/add | solution.py:379
  177.2 4.1 %all-to-all-start.2 = ((f32[4,8,16,512]{3,2,1,0:T(8,128)}), f32[4,8,16,512]{3,2,1,0:T(8,128)S(1)}, u32[]{:S(2)}, u32[]{:S(2)}) async-start(f32[4,8,16,512]{3,2,1,0:T(8,128)} %add.87), calls=%async_computation.2 | async-start | bytes 2097152 | tf_op jit(solution)/shard_map/all_to_all | solution.py:379
  181.3 3.2 %collective-permute-start.18 = (f32[8,256]{1,0:T(8,128)S(1)}, f32[8,256]{1,0:T(8,128)S(1)}, u32[]{:S(2)}, u32[]{:S(2)}) collective-permute-start(f32[8,256]{1,0:T(8,128)S(1)} %constant_dynamic-update-slice_fusion), channel_id=1, source_target_pairs={{0,128},{64,192},{128,0},{192,64},{1,129},{65,193},{129,1},{193,65... | collective-permute-start | bytes 24584 | tf_op jit(solution)/shard_map/ppermute | solution.py:316
  184.6 5.6 %shard_map.96 = bf16[896,1280]{1,0:T(8,128)(2,1)} custom-call(bf16[896,1024]{1,0:T(8,128)(2,1)} %copy-done.2, bf16[128,1280]{1,0:T(8,128)(2,1)S(1)} %collective-permute-done.10.far.refs_0_, bf16[128,1280]{1,0:T(8,128)(2,1)S(1)} %collective-permute-done.11.after.refs_1_, bf16[128,1280]{1,0:T(8,128)(2,1)S(1)} %collective-permute-done.12.before.refs_2_, ...), custom_call_target="tpu_custom_call" | custom-call | tf_op jit(solution)/shard_map/pallas_call | solution.py:32
  190.2 5.7 %all-to-all-done.2 = f32[4,8,16,512]{3,2,1,0:T(8,128)S(1)} async-done(((f32[4,8,16,512]{3,2,1,0:T(8,128)}), f32[4,8,16,512]{3,2,1,0:T(8,128)S(1)}, u32[]{:S(2)}, u32[]{:S(2)}) %all-to-all-start.2) | async-done | bytes 1048608 | tf_op jit(solution)/shard_map/all_to_all | solution.py:379
  196.8 3.9 %all-to-all-start.3 = ((f32[8,32,512]{2,1,0:T(8,128)}), f32[8,32,512]{2,1,0:T(8,128)S(1)}, u32[]{:S(2)}, u32[]{:S(2)}) async-start(f32[8,32,512]{2,1,0:T(8,128)} %pad_maximum_fusion), calls=%async_computation.3 | async-start | bytes 1048576 | tf_op jit(solution)/shard_map/all_to_all | solution.py:385
  201.5 15.1 %all-to-all-done.3 = f32[8,32,512]{2,1,0:T(8,128)S(1)} async-done(((f32[8,32,512]{2,1,0:T(8,128)}), f32[8,32,512]{2,1,0:T(8,128)S(1)}, u32[]{:S(2)}, u32[]{:S(2)}) %all-to-all-start.3) | async-done | bytes 524320 | tf_op jit(solution)/shard_map/all_to_all | solution.py:385
  216.7 2.6 %collective-permute-start.21 = (bf16[16,512]{1,0:T(8,128)(2,1)S(1)}, bf16[16,512]{1,0:T(8,128)(2,1)S(1)}, u32[]{:S(2)}, u32[]{:S(2)}) collective-permute-start(bf16[16,512]{1,0:T(8,128)(2,1)S(1)} %broadcast_select_fusion.1), channel_id=1, source_target_pairs={{0,1},{1,0},{2,3},{3,2},{4,5},{5,4},{6,7},{7,6},{8,9},{9,8},{10,11... | collective-permute-start | bytes 49160 | tf_op jit(solution)/shard_map/ppermute | solution.py:316
  (99 shorter events, 31.3 us)
Async XLA Ops:
  0.6 10.7 %copy-start.13 = (s32[8,64]{1,0:T(8,128)S(1)}, s32[8,64]{1,0:T(8,128)}, u32[]{:S(2)}) copy-start(s32[8,64]{1,0:T(8,128)} %param.10) | copy-start | bytes 6148
  8.1 15.5 %collective-permute-start = (f32[2,128,640]{2,1,0:T(8,128)S(1)}, f32[2,128,640]{2,1,0:T(8,128)S(1)}, u32[]{:S(2)}, u32[]{:S(2)}) collective-permute-start(f32[2,128,640]{2,1,0:T(8,128)S(1)} %get-tuple-element.74), channel_id=1, source_target_pairs={{0,64},{64,128},{128,192},{192,0},{1,65},{65,129},{129,193},{193,1... | collective-permute-start | bytes 1966088 | tf_op jit(solution)/shard_map/ppermute | solution.py:316
  10.1 15.0 %collective-permute-start.1 = (f32[2,128,640]{2,1,0:T(8,128)S(1)}, f32[2,128,640]{2,1,0:T(8,128)S(1)}, u32[]{:S(2)}, u32[]{:S(2)}) collective-permute-start(f32[2,128,640]{2,1,0:T(8,128)S(1)} %get-tuple-element.75), channel_id=1, source_target_pairs={{0,192},{64,0},{128,64},{192,128},{1,193},{65,1},{129,65},{193,129... | collective-permute-start | bytes 1966088 | tf_op jit(solution)/shard_map/ppermute | solution.py:316
  22.1 28.1 %copy-start.5 = (f32[128,1280]{1,0:T(8,128)S(1)}, f32[128,1280]{1,0:T(8,128)}, u32[]{:S(2)}) copy-start(f32[128,1280]{1,0:T(8,128)} %get-tuple-element.86.nxt) | copy-start | bytes 1966084
  27.6 27.7 %collective-permute-start.8 = (f32[128,1280]{1,0:T(8,128)S(1)}, f32[128,1280]{1,0:T(8,128)S(1)}, u32[]{:S(2)}, u32[]{:S(2)}) collective-permute-start(f32[128,1280]{1,0:T(8,128)S(1)} %get-tuple-element.76), channel_id=1, source_target_pairs={{0,64},{64,128},{128,192},{192,0},{1,65},{65,129},{129,193},{193,1... | collective-permute-start | bytes 1966088 | tf_op jit(solution)/shard_map/ppermute | solution.py:316
  29.1 18.8 %collective-permute-start.2 = (f32[2,128,256]{2,1,0:T(8,128)S(1)}, f32[2,128,256]{2,1,0:T(8,128)S(1)}, u32[]{:S(2)}, u32[]{:S(2)}) collective-permute-start(f32[2,128,256]{2,1,0:T(8,128)S(1)} %get-tuple-element.81), channel_id=1, source_target_pairs={{0,64},{64,128},{128,192},{192,0},{1,65},{65,129},{129,193},{193,1... | collective-permute-start | bytes 786440 | tf_op jit(solution)/shard_map/ppermute | solution.py:316
  30.3 17.7 %collective-permute-start.3 = (f32[2,128,256]{2,1,0:T(8,128)S(1)}, f32[2,128,256]{2,1,0:T(8,128)S(1)}, u32[]{:S(2)}, u32[]{:S(2)}) collective-permute-start(f32[2,128,256]{2,1,0:T(8,128)S(1)} %get-tuple-element.82), channel_id=1, source_target_pairs={{0,192},{64,0},{128,64},{192,128},{1,193},{65,1},{129,65},{193,129... | collective-permute-start | bytes 786440 | tf_op jit(solution)/shard_map/ppermute | solution.py:316
  31.8 33.3 %collective-permute-start.9 = (f32[128,1280]{1,0:T(8,128)S(1)}, f32[128,1280]{1,0:T(8,128)}, u32[]{:S(2)}, u32[]{:S(2)}) collective-permute-start(f32[128,1280]{1,0:T(8,128)S(1)} %get-tuple-element.96), channel_id=1, source_target_pairs={{0,192},{64,0},{128,64},{192,128},{1,193},{65,1},{129,65},{193,129... | collective-permute-start | bytes 1966088 | tf_op jit(solution)/shard_map/ppermute | solution.py:316
  52.6 25.8 %copy-start = (f32[2,128,512]{2,1,0:T(8,128)S(1)}, f32[2,128,512]{2,1,0:T(8,128)}, u32[]{:S(2)}) copy-start(f32[2,128,512]{2,1,0:T(8,128)} %get-tuple-element.69.town) | copy-start | bytes 1572868
  52.6 28.7 %collective-permute-start.4 = (f32[128,1280]{1,0:T(8,128)}, f32[128,1280]{1,0:T(8,128)}, u32[]{:S(2)}, u32[]{:S(2)}) collective-permute-start(f32[128,1280]{1,0:T(8,128)} %get-tuple-element.88), channel_id=1, source_target_pairs={{0,64},{64,128},{128,192},{192,0},{1,65},{65,129},{129,193},{193,1... | collective-permute-start | bytes 1966088 | tf_op jit(solution)/shard_map/ppermute | solution.py:316
  53.8 27.4 %collective-permute-start.5 = (f32[128,1280]{1,0:T(8,128)S(1)}, f32[128,1280]{1,0:T(8,128)}, u32[]{:S(2)}, u32[]{:S(2)}) collective-permute-start(f32[128,1280]{1,0:T(8,128)S(1)} %get-tuple-element.92), channel_id=1, source_target_pairs={{0,192},{64,0},{128,64},{192,128},{1,193},{65,1},{129,65},{193,129... | collective-permute-start | bytes 1966088 | tf_op jit(solution)/shard_map/ppermute | solution.py:316
  55.3 22.5 %collective-permute-start.6 = (f32[2,128,512]{2,1,0:T(8,128)}, f32[2,128,512]{2,1,0:T(8,128)S(1)}, u32[]{:S(2)}, u32[]{:S(2)}) collective-permute-start(f32[2,128,512]{2,1,0:T(8,128)} %get-tuple-element.83), channel_id=1, source_target_pairs={{0,64},{64,128},{128,192},{192,0},{1,65},{65,129},{129,193},{193,1... | collective-permute-start | bytes 1572872 | tf_op jit(solution)/shard_map/ppermute | solution.py:316
  56.1 22.2 %collective-permute-start.7 = (f32[2,128,512]{2,1,0:T(8,128)}, f32[2,128,512]{2,1,0:T(8,128)S(1)}, u32[]{:S(2)}, u32[]{:S(2)}) collective-permute-start(f32[2,128,512]{2,1,0:T(8,128)} %get-tuple-element.93), channel_id=1, source_target_pairs={{0,192},{64,0},{128,64},{192,128},{1,193},{65,1},{129,65},{193,129... | collective-permute-start | bytes 1572872 | tf_op jit(solution)/shard_map/ppermute | solution.py:316
  81.3 34.4 %copy-start.7 = (f32[128,1280]{1,0:T(8,128)S(1)}, f32[128,1280]{1,0:T(8,128)}, u32[]{:S(2)}) copy-start(f32[128,1280]{1,0:T(8,128)} %get-tuple-element.104.e_in) | copy-start | bytes 1966084
  84.1 35.7 %copy-start.6 = (f32[128,1280]{1,0:T(8,128)S(1)}, f32[128,1280]{1,0:T(8,128)}, u32[]{:S(2)}) copy-start(f32[128,1280]{1,0:T(8,128)} %get-tuple-element.101.e_in) | copy-start | bytes 1966084
  116.8 10.5 %collective-permute-start.10 = (bf16[128,1280]{1,0:T(8,128)(2,1)S(1)}, bf16[128,1280]{1,0:T(8,128)(2,1)S(1)}, u32[]{:S(2)}, u32[]{:S(2)}) collective-permute-start(bf16[128,1280]{1,0:T(8,128)(2,1)S(1)} %get-tuple-element.112.own.refs_3_), channel_id=1, source_target_pairs={{0,128},{64,192},{128,0},{192,64},{1,129},{65,193},{129,1},{193,65... | collective-permute-start | bytes 983048 | tf_op jit(solution)/shard_map/ppermute | solution.py:316
  117.8 16.6 %collective-permute-start.11 = (bf16[128,1280]{1,0:T(8,128)(2,1)S(1)}, bf16[128,1280]{1,0:T(8,128)(2,1)S(1)}, u32[]{:S(2)}, u32[]{:S(2)}) collective-permute-start(bf16[128,1280]{1,0:T(8,128)(2,1)S(1)} %get-tuple-element.112.own.refs_3_), channel_id=1, source_target_pairs={{0,192},{64,0},{128,64},{192,128},{1,193},{65,1},{129,65},{193,129... | collective-permute-start | bytes 983048 | tf_op jit(solution)/shard_map/ppermute | solution.py:316
  119.4 15.6 %collective-permute-start.12 = (bf16[128,1280]{1,0:T(8,128)(2,1)S(1)}, bf16[128,1280]{1,0:T(8,128)(2,1)S(1)}, u32[]{:S(2)}, u32[]{:S(2)}) collective-permute-start(bf16[128,1280]{1,0:T(8,128)(2,1)S(1)} %get-tuple-element.112.own.refs_3_), channel_id=1, source_target_pairs={{0,64},{64,128},{128,192},{192,0},{1,65},{65,129},{129,193},{193,1... | collective-permute-start | bytes 983048 | tf_op jit(solution)/shard_map/ppermute | solution.py:316
  121.0 46.4 %copy-start.3 = (bf16[128,1280]{1,0:T(8,128)(2,1)}, bf16[128,1280]{1,0:T(8,128)(2,1)S(1)}, u32[]{:S(2)}) copy-start(bf16[128,1280]{1,0:T(8,128)(2,1)S(1)} %get-tuple-element.118.refs_7_.own) | copy-start | bytes 983044
  139.3 3.1 %collective-permute-start.13 = (f32[4,8,16,512]{3,2,1,0:T(8,128)}, f32[4,8,16,512]{3,2,1,0:T(8,128)S(1)}, u32[]{:S(2)}, u32[]{:S(2)}) collective-permute-start(f32[4,8,16,512]{3,2,1,0:T(8,128)} %get-tuple-element.114), channel_id=1, source_target_pairs={{0,1},{1,0},{2,3},{3,2},{4,5},{5,4},{6,7},{7,6},{8,9},{9,8},{10,11... | collective-permute-start | bytes 3145736 | tf_op jit(solution)/shard_map/ppermute | solution.py:316
  144.9 19.2 %all-to-all-start.1 = ((f32[4,8,16,512]{3,2,1,0:T(8,128)}), f32[4,8,16,512]{3,2,1,0:T(8,128)}, u32[]{:S(2)}, u32[]{:S(2)}) async-start(f32[4,8,16,512]{3,2,1,0:T(8,128)} %add.86), calls=%async_computation.1 | async-start | bytes 2097152 | tf_op jit(solution)/shard_map/all_to_all | solution.py:375
  149.1 16.2 %collective-permute-start.14 = (bf16[128,1280]{1,0:T(8,128)(2,1)S(1)}, bf16[128,1280]{1,0:T(8,128)(2,1)S(1)}, u32[]{:S(2)}, u32[]{:S(2)}) collective-permute-start(bf16[128,1280]{1,0:T(8,128)(2,1)S(1)} %get-tuple-element.118.refs_7_.own), channel_id=1, source_target_pairs={{0,128},{64,192},{128,0},{192,64},{1,129},{65,193},{129,1},{193,65... | collective-permute-start | bytes 983048 | tf_op jit(solution)/shard_map/ppermute | solution.py:316
  150.1 16.4 %collective-permute-start.15 = (bf16[128,1280]{1,0:T(8,128)(2,1)S(1)}, bf16[128,1280]{1,0:T(8,128)(2,1)S(1)}, u32[]{:S(2)}, u32[]{:S(2)}) collective-permute-start(bf16[128,1280]{1,0:T(8,128)(2,1)S(1)} %get-tuple-element.118.refs_7_.own), channel_id=1, source_target_pairs={{0,192},{64,0},{128,64},{192,128},{1,193},{65,1},{129,65},{193,129... | collective-permute-start | bytes 983048 | tf_op jit(solution)/shard_map/ppermute | solution.py:316
  151.6 15.8 %collective-permute-start.16 = (bf16[128,1280]{1,0:T(8,128)(2,1)S(1)}, bf16[128,1280]{1,0:T(8,128)(2,1)S(1)}, u32[]{:S(2)}, u32[]{:S(2)}) collective-permute-start(bf16[128,1280]{1,0:T(8,128)(2,1)S(1)} %get-tuple-element.118.refs_7_.own), channel_id=1, source_target_pairs={{0,64},{64,128},{128,192},{192,0},{1,65},{65,129},{129,193},{193,1... | collective-permute-start | bytes 983048 | tf_op jit(solution)/shard_map/ppermute | solution.py:316
  167.4 9.8 %copy-start.4 = (bf16[128,1280]{1,0:T(8,128)(2,1)}, bf16[128,1280]{1,0:T(8,128)(2,1)S(1)}, u32[]{:S(2)}) copy-start(bf16[128,1280]{1,0:T(8,128)(2,1)S(1)} %collective-permute-done.16.refs_6_.before) | copy-start | bytes 983044
  171.8 3.0 %collective-permute-start.20 = (f32[4,8,16,512]{3,2,1,0:T(8,128)}, f32[4,8,16,512]{3,2,1,0:T(8,128)S(1)}, u32[]{:S(2)}, u32[]{:S(2)}) collective-permute-start(f32[4,8,16,512]{3,2,1,0:T(8,128)} %get-tuple-element.122), channel_id=1, source_target_pairs={{0,1},{1,0},{2,3},{3,2},{4,5},{5,4},{6,7},{7,6},{8,9},{9,8},{10,11... | collective-permute-start | bytes 3145736 | tf_op jit(solution)/shard_map/ppermute | solution.py:316
  177.2 18.6 %all-to-all-start.2 = ((f32[4,8,16,512]{3,2,1,0:T(8,128)}), f32[4,8,16,512]{3,2,1,0:T(8,128)S(1)}, u32[]{:S(2)}, u32[]{:S(2)}) async-start(f32[4,8,16,512]{3,2,1,0:T(8,128)} %add.87), calls=%async_computation.2 | async-start | bytes 2097152 | tf_op jit(solution)/shard_map/all_to_all | solution.py:379
  181.3 8.8 %collective-permute-start.17 = (f32[8,256]{1,0:T(8,128)S(1)}, f32[8,256]{1,0:T(8,128)S(1)}, u32[]{:S(2)}, u32[]{:S(2)}) collective-permute-start(f32[8,256]{1,0:T(8,128)S(1)} %constant_dynamic-update-slice_fusion), channel_id=1, source_target_pairs={{0,64},{64,128},{128,192},{192,0},{1,65},{65,129},{129,193},{193,1... | collective-permute-start | bytes 24584 | tf_op jit(solution)/shard_map/ppermute | solution.py:316
  181.3 8.8 %collective-permute-start.18 = (f32[8,256]{1,0:T(8,128)S(1)}, f32[8,256]{1,0:T(8,128)S(1)}, u32[]{:S(2)}, u32[]{:S(2)}) collective-permute-start(f32[8,256]{1,0:T(8,128)S(1)} %constant_dynamic-update-slice_fusion), channel_id=1, source_target_pairs={{0,128},{64,192},{128,0},{192,64},{1,129},{65,193},{129,1},{193,65... | collective-permute-start | bytes 24584 | tf_op jit(solution)/shard_map/ppermute | solution.py:316
  184.6 5.6 %collective-permute-start.19 = (f32[8,256]{1,0:T(8,128)S(1)}, f32[8,256]{1,0:T(8,128)S(1)}, u32[]{:S(2)}, u32[]{:S(2)}) collective-permute-start(f32[8,256]{1,0:T(8,128)S(1)} %constant_dynamic-update-slice_fusion), channel_id=1, source_target_pairs={{0,192},{64,0},{128,64},{192,128},{1,193},{65,1},{129,65},{193,129... | collective-permute-start | bytes 24584 | tf_op jit(solution)/shard_map/ppermute | solution.py:316
  196.8 19.8 %all-to-all-start.3 = ((f32[8,32,512]{2,1,0:T(8,128)}), f32[8,32,512]{2,1,0:T(8,128)S(1)}, u32[]{:S(2)}, u32[]{:S(2)}) async-start(f32[8,32,512]{2,1,0:T(8,128)} %pad_maximum_fusion), calls=%async_computation.3 | async-start | bytes 1048576 | tf_op jit(solution)/shard_map/all_to_all | solution.py:385
  216.7 3.4 %collective-permute-start.21 = (bf16[16,512]{1,0:T(8,128)(2,1)S(1)}, bf16[16,512]{1,0:T(8,128)(2,1)S(1)}, u32[]{:S(2)}, u32[]{:S(2)}) collective-permute-start(bf16[16,512]{1,0:T(8,128)(2,1)S(1)} %broadcast_select_fusion.1), channel_id=1, source_target_pairs={{0,1},{1,0},{2,3},{3,2},{4,5},{5,4},{6,7},{7,6},{8,9},{9,8},{10,11... | collective-permute-start | bytes 49160 | tf_op jit(solution)/shard_map/ppermute | solution.py:316
  (7 other events, 9.1 us)
